TPU v7x, 32 devices: a whole 2x2x4 slice. The times are simulated.
32 devices in a mesh: tile: 8 (over y, x, core), member: 4 (over z).
Axes of the slice: x: 2, y: 2, z: 4, core: 2. Of those that a mesh axis runs over, the one named last changes fastest.
Arguments:
- residual_in: float32 [64, 128, 512], P(None, 'tile', 'member'), may hold values from -6 to 6
- members: bfloat16 [8, 64, 128, 512], P('member', None, 'tile'), may hold values from -6 to 6
- wind_x: float32 [64], replicated, may hold values from 0.05 to 0.25
- wind_y: float32 [64], replicated, may hold values from 0.05 to 0.25
Outputs:
- analysis: float32 [64, 128, 512], P(None, 'tile', 'member')
- residual: float32 [64, 128, 512], P(None, 'tile', 'member')
All inputs are finite; a program needn't handle non-finite values.
Results may differ from a plain program's by a relative error of at most 0.006.
Values may be sent and summed in bfloat16 or wider, within the bound.
No kernel may reach another device: no remote copies, remote signals or barrier semaphores. Data moves between devices by JAX's collectives and lax.ppermute only.
A program may use at most 64 MiB of HBM per device.

v0:
```python
import jax
import jax.numpy as jnp
from jax import lax
from jax.sharding import PartitionSpec as P

ITERS = 2
MODEL_STEPS = 4


diffusion = 0.1
relax = 0.5


def padded_2(block, sides, width):
    for axis, dim in sides:
        count = lax.axis_size(axis)
        forward = [(i, i + 1) for i in range(count - 1)]
        backward = [(target, source) for source, target in forward]
        low = lax.ppermute(
            lax.slice_in_dim(block, block.shape[dim] - width, None, axis=dim), axis, forward
        )
        high = lax.ppermute(lax.slice_in_dim(block, 0, width, axis=dim), axis, backward)
        block = jnp.concatenate([low, block, high], axis=dim)
    return block


def taper_weights():
    raw = [1.0 - (k / 17.0) ** 2 for k in range(-16, 17)]
    total = sum(raw)
    return [value / total for value in raw]


def advance(padded, wind_x, wind_y):
    center = padded[:, 1:-1, 1:-1]
    ahead_x = padded[:, 2:, 1:-1]
    behind_x = padded[:, :-2, 1:-1]
    ahead_y = padded[:, 1:-1, 2:]
    behind_y = padded[:, 1:-1, :-2]
    result = center + diffusion * (ahead_x + behind_x + ahead_y + behind_y - 4.0 * center)
    result = result - wind_x[:, None, None] * (center - ahead_x)
    return result - wind_y[:, None, None] * (center - ahead_y)


def smooth_axis(padded, count, axis):
    weights = taper_weights()
    total = weights[0] * lax.slice_in_dim(padded, 0, count, axis=axis)
    for offset in range(1, len(weights)):
        total = total + weights[offset] * lax.slice_in_dim(
            padded, offset, offset + count, axis=axis
        )
    return total


def adjoint_model(field, wind_x, wind_y):
    for sweep in range(MODEL_STEPS):
        padded = padded_2(field, (("tile", 1), ("member", 2)), 1)
        field = advance(padded, wind_x, wind_y)
    return field


def per_device(residual_in, members, wind_x, wind_y):
    residual = residual_in
    analysis = jnp.zeros_like(residual_in)
    block_rows = residual_in.shape[1]
    block_cols = residual_in.shape[2]
    block_members = lax.all_to_all(members, "member", split_axis=3, concat_axis=0, tiled=True)
    block_members_f = block_members.astype(jnp.float32)
    for iteration in range(ITERS):
        grad = adjoint_model(residual, wind_x, wind_y).astype(jnp.bfloat16).astype(jnp.float32)
        project = jnp.sum(block_members_f * grad[None], axis=1)
        padded_all = padded_2(project, (("tile", 1), ("member", 2)), 16)
        smoothed = smooth_axis(padded_all, block_rows, 1)
        localized = smooth_axis(smoothed, block_cols, 2)
        increment = jnp.sum(block_members_f * localized[:, None], axis=0)
        analysis = analysis + increment
        residual = residual - relax * increment
    return (analysis, residual)


def solution(mesh):
    return jax.shard_map(
        per_device,
        mesh=mesh,
        in_specs=(P(None, "tile", "member"), P("member", None, "tile", None), P(), P()),
        out_specs=(P(None, "tile", "member"), P(None, "tile", "member")),
        check_vma=False,
    )
```

profile of v0, /device:TPU:20, one launch (start us, length us, event | category | flops | bytes accessed | tf_op | source)
XLA Modules:
  0.0 299.8 jit_solution(16105839693814256052)
XLA Ops:
  6.4 8.6 %copy.170 = bf16[2,64,16,512]{1,2,0,3:T(8,128)(2,1)} copy(bf16[2,64,16,512]{3,2,1,0:T(8,128)(2,1)} %param.5) | data formatting | bytes 4194304 | tf_op args[1]
  15.1 6.0 %reshape.19 = bf16[4,2,131072]{2,1,0:T(2,128)(2,1)} reshape(bf16[512,2,16,64]{3,2,1,0:T(8,128)(2,1)} %bitcast.21) | data formatting | bytes 4194304
  21.0 5.2 %all-to-all-start = ((bf16[4,2,131072]{2,1,0:T(2,128)(2,1)}), bf16[4,2,131072]{2,1,0:T(2,128)(2,1)S(1)}, u32[]{:S(2)}, u32[]{:S(2)}) async-start(bf16[4,2,131072]{2,1,0:T(2,128)(2,1)} %reshape.19), calls=%async_computation | async-start | bytes 4194304 | tf_op jit(solution)/shard_map/all_to_all | solution.py:66
  29.0 3.4 %collective-permute-start.3 = (f32[64,18,1]{0,1,2:T(8,128)S(1)}, f32[64,18,1]{0,1,2:T(8,128)S(1)}, u32[]{:S(2)}, u32[]{:S(2)}) collective-permute-start(f32[64,18,1]{0,1,2:T(8,128)S(1)} %copy.174), channel_id=1, source_target_pairs={{0,1},{1,2},{2,3},{4,5},{5,6},{6,7},{8,9},{9,10},{10,11},{12,13},{... | collective-permute-start | bytes 13832 | tf_op jit(solution)/shard_map/ppermute | solution.py:19
  35.2 38.1 %collective-permute-done.3 = f32[64,18,1]{0,1,2:T(8,128)S(1)} collective-permute-done((f32[64,18,1]{0,1,2:T(8,128)S(1)}, f32[64,18,1]{0,1,2:T(8,128)S(1)}, u32[]{:S(2)}, u32[]{:S(2)}) %collective-permute-start.3) | collective-permute-done | bytes 4640 | tf_op jit(solution)/shard_map/ppermute | solution.py:19
  76.8 2.9 collective-permute-start.4
  81.7 4.2 %collective-permute-done.5 = f32[64,1,128]{2,1,0:T(1,128)S(1)} collective-permute-done((f32[64,1,128]{2,1,0:T(1,128)S(1)}, f32[64,1,128]{2,1,0:T(1,128)S(1)}, u32[]{:S(2)}, u32[]{:S(2)}) %collective-permute-start.5) | collective-permute-done | bytes 32800 | tf_op jit(solution)/shard_map/ppermute | solution.py:19
  90.9 3.9 %collective-permute-start.6 = (f32[64,18,1]{0,1,2:T(8,128)S(1)}, f32[64,18,1]{0,1,2:T(8,128)S(1)}, u32[]{:S(2)}, u32[]{:S(2)}) collective-permute-start(f32[64,18,1]{0,1,2:T(8,128)S(1)} %copy.176), channel_id=1, source_target_pairs={{1,0},{2,1},{3,2},{5,4},{6,5},{7,6},{9,8},{10,9},{11,10},{13,12},{... | collective-permute-start | bytes 13832 | tf_op jit(solution)/shard_map/ppermute | solution.py:22
  97.7 3.4 %fusion.71 = f32[64,16,128]{2,1,0:T(8,128)S(1)} fusion(f32[64,16,128]{2,1,0:T(8,128)} %copy-done.4, f32[64,18,1]{2,1,0:T(8,128)} %copy.179, f32[64,1,128]{2,1,0:T(1,128)S(1)} %collective-permute-done.4, f32[64,1,128]{2,1,0:T(1,128)S(1)} %collective-permute-done.5, f32[64,18,1]{2,1,0:T(8,128)} %copy.177, f32[64]{0:T(128)S(1)} %copy-done.6, f32[64]{0:T(128)S(1)} %copy-done.7), kind=kLoop, calls=%fused_computation.132 | loop fusion | flops 2752512 | bytes 1123840 | tf_op jit(solution)/shard_map/sub | solution.py:41
  105.4 3.7 %collective-permute-done.9 = f32[64,1,128]{2,1,0:T(1,128)S(1)} collective-permute-done((f32[64,1,128]{2,1,0:T(1,128)S(1)}, f32[64,1,128]{2,1,0:T(1,128)S(1)}, u32[]{:S(2)}, u32[]{:S(2)}) %collective-permute-start.9) | collective-permute-done | bytes 32800 | tf_op jit(solution)/shard_map/ppermute | solution.py:19
  115.4 3.9 %collective-permute-start.10 = (f32[64,18,1]{0,1,2:T(8,128)S(1)}, f32[64,18,1]{0,1,2:T(8,128)S(1)}, u32[]{:S(2)}, u32[]{:S(2)}) collective-permute-start(f32[64,18,1]{0,1,2:T(8,128)S(1)} %copy.180), channel_id=1, source_target_pairs={{1,0},{2,1},{3,2},{5,4},{6,5},{7,6},{9,8},{10,9},{11,10},{13,12},{... | collective-permute-start | bytes 13832 | tf_op jit(solution)/shard_map/ppermute | solution.py:22
  128.8 3.7 %collective-permute-done.13 = f32[64,1,128]{2,1,0:T(1,128)S(1)} collective-permute-done((f32[64,1,128]{2,1,0:T(1,128)S(1)}, f32[64,1,128]{2,1,0:T(1,128)S(1)}, u32[]{:S(2)}, u32[]{:S(2)}) %collective-permute-start.13) | collective-permute-done | bytes 32800 | tf_op jit(solution)/shard_map/ppermute | solution.py:19
  137.5 4.1 %collective-permute-start.14 = (f32[64,18,1]{0,1,2:T(8,128)S(1)}, f32[64,18,1]{0,1,2:T(8,128)S(1)}, u32[]{:S(2)}, u32[]{:S(2)}) collective-permute-start(f32[64,18,1]{0,1,2:T(8,128)S(1)} %copy.184), channel_id=1, source_target_pairs={{1,0},{2,1},{3,2},{5,4},{6,5},{7,6},{9,8},{10,9},{11,10},{13,12},{... | collective-permute-start | bytes 13832 | tf_op jit(solution)/shard_map/ppermute | solution.py:22
  144.3 4.0 %fusion.86 = f32[64,16,128]{2,1,0:T(8,128)} fusion(f32[64,16,128]{2,1,0:T(8,128)} %copy-done.3, f32[64]{0:T(128)S(1)} %copy-done.6, f32[64]{0:T(128)S(1)} %copy-done.7, f32[64,1,128]{2,1,0:T(1,128)S(1)} %collective-permute-done.12, f32[64,1,128]{2,1,0:T(1,128)S(1)} %collective-permute-done.13, f32[64,18,1]{2,1,0:T(8,128)S(1)} %copy.187, f32[64,18,1]{2,1,0:T(8,128)} %copy.185), kind=kLoop, calls=%fused_computation.166 | loop fusion | flops 3014656 | bytes 1123840 | tf_op jit(solution)/shard_map/convert_element_type | solution.py:69
  148.3 4.0 %reshape.20 = bf16[512,2,16,64]{3,2,1,0:T(8,128)(2,1)} reshape(bf16[4,2,131072]{2,1,0:T(2,128)(2,1)S(1)} %all-to-all-done) | data formatting | bytes 4194304
  152.3 7.3 %copy.171 = f32[2,64,16,4,128]{4,3,2,1,0:T(4,128)} copy(bf16[2,64,16,4,128]{1,2,0,4,3:T(8,128)(2,1)} %bitcast.22) | data formatting | bytes 6291456 | tf_op jit(solution)/shard_map/convert_element_type | solution.py:67
  159.6 3.2 %fusion = f32[4,2,16,128]{3,0,2,1:T(4,128)S(1)} fusion(f32[2,64,16,4,128]{4,3,2,1,0:T(4,128)} %copy.171, f32[64,16,128]{2,1,0:T(8,128)S(1)} %copy-done.5), kind=kLoop, calls=%fused_computation.4 | loop fusion | flops 2080768 | bytes 4784128 | tf_op jit(solution)/shard_map/reduce_sum | solution.py:70
  167.2 4.1 %collective-permute-done.16 = f32[8,16,128]{2,1,0:T(8,128)S(1)} collective-permute-done((f32[8,16,128]{2,1,0:T(8,128)S(1)}, f32[8,16,128]{2,1,0:T(8,128)S(1)}, u32[]{:S(2)}, u32[]{:S(2)}) %collective-permute-start.16) | collective-permute-done | bytes 65568 | tf_op jit(solution)/shard_map/ppermute | solution.py:19
  171.4 4.2 %collective-permute-start.19 = (f32[8,48,16]{2,1,0:T(8,128)S(1)}, f32[8,48,16]{2,1,0:T(8,128)S(1)}, u32[]{:S(2)}, u32[]{:S(2)}) collective-permute-start(f32[8,48,16]{2,1,0:T(8,128)S(1)} %get-tuple-element.43), channel_id=1, source_target_pairs={{1,0},{2,1},{3,2},{5,4},{6,5},{7,6},{9,8},{10,9},{11,10},{13,12},{... | collective-permute-start | bytes 73736 | tf_op jit(solution)/shard_map/ppermute | solution.py:22
  179.2 3.9 %collective-permute-done.18 = f32[8,48,16]{2,1,0:T(8,128)S(1)} collective-permute-done((f32[8,48,16]{2,1,0:T(8,128)S(1)}, f32[8,48,16]{2,1,0:T(8,128)S(1)}, u32[]{:S(2)}, u32[]{:S(2)}) %collective-permute-start.18) | collective-permute-done | bytes 24608 | tf_op jit(solution)/shard_map/ppermute | solution.py:19
  191.0 3.7 %collective-permute-done.21 = f32[64,1,128]{2,1,0:T(1,128)S(1)} collective-permute-done((f32[64,1,128]{2,1,0:T(1,128)S(1)}, f32[64,1,128]{2,1,0:T(1,128)S(1)}, u32[]{:S(2)}, u32[]{:S(2)}) %collective-permute-start.21) | collective-permute-done | bytes 32800 | tf_op jit(solution)/shard_map/ppermute | solution.py:19
  197.7 3.9 %collective-permute-start.22 = (f32[64,18,1]{0,1,2:T(8,128)S(1)}, f32[64,18,1]{0,1,2:T(8,128)S(1)}, u32[]{:S(2)}, u32[]{:S(2)}) collective-permute-start(f32[64,18,1]{0,1,2:T(8,128)S(1)} %copy.190), channel_id=1, source_target_pairs={{1,0},{2,1},{3,2},{5,4},{6,5},{7,6},{9,8},{10,9},{11,10},{13,12},{... | collective-permute-start | bytes 13832 | tf_op jit(solution)/shard_map/ppermute | solution.py:22
  210.8 3.7 %collective-permute-done.25 = f32[64,1,128]{2,1,0:T(1,128)S(1)} collective-permute-done((f32[64,1,128]{2,1,0:T(1,128)S(1)}, f32[64,1,128]{2,1,0:T(1,128)S(1)}, u32[]{:S(2)}, u32[]{:S(2)}) %collective-permute-start.25) | collective-permute-done | bytes 32800 | tf_op jit(solution)/shard_map/ppermute | solution.py:19
  219.5 4.1 %collective-permute-start.26 = (f32[64,18,1]{0,1,2:T(8,128)S(1)}, f32[64,18,1]{0,1,2:T(8,128)S(1)}, u32[]{:S(2)}, u32[]{:S(2)}) collective-permute-start(f32[64,18,1]{0,1,2:T(8,128)S(1)} %copy.194), channel_id=1, source_target_pairs={{1,0},{2,1},{3,2},{5,4},{6,5},{7,6},{9,8},{10,9},{11,10},{13,12},{... | collective-permute-start | bytes 13832 | tf_op jit(solution)/shard_map/ppermute | solution.py:22
  232.6 3.7 %collective-permute-done.29 = f32[64,1,128]{2,1,0:T(1,128)S(1)} collective-permute-done((f32[64,1,128]{2,1,0:T(1,128)S(1)}, f32[64,1,128]{2,1,0:T(1,128)S(1)}, u32[]{:S(2)}, u32[]{:S(2)}) %collective-permute-start.29) | collective-permute-done | bytes 32800 | tf_op jit(solution)/shard_map/ppermute | solution.py:19
  241.3 3.9 %collective-permute-start.30 = (f32[64,18,1]{0,1,2:T(8,128)S(1)}, f32[64,18,1]{0,1,2:T(8,128)S(1)}, u32[]{:S(2)}, u32[]{:S(2)}) collective-permute-start(f32[64,18,1]{0,1,2:T(8,128)S(1)} %copy.198), channel_id=1, source_target_pairs={{1,0},{2,1},{3,2},{5,4},{6,5},{7,6},{9,8},{10,9},{11,10},{13,12},{... | collective-permute-start | bytes 13832 | tf_op jit(solution)/shard_map/ppermute | solution.py:22
  254.4 3.7 %collective-permute-done.33 = f32[64,1,128]{2,1,0:T(1,128)S(1)} collective-permute-done((f32[64,1,128]{2,1,0:T(1,128)S(1)}, f32[64,1,128]{2,1,0:T(1,128)S(1)}, u32[]{:S(2)}, u32[]{:S(2)}) %collective-permute-start.33) | collective-permute-done | bytes 32800 | tf_op jit(solution)/shard_map/ppermute | solution.py:19
  263.1 3.9 %collective-permute-start.34 = (f32[64,18,1]{0,1,2:T(8,128)S(1)}, f32[64,18,1]{0,1,2:T(8,128)S(1)}, u32[]{:S(2)}, u32[]{:S(2)}) collective-permute-start(f32[64,18,1]{0,1,2:T(8,128)S(1)} %copy.202), channel_id=1, source_target_pairs={{1,0},{2,1},{3,2},{5,4},{6,5},{7,6},{9,8},{10,9},{11,10},{13,12},{... | collective-permute-start | bytes 13832 | tf_op jit(solution)/shard_map/ppermute | solution.py:22
  271.8 3.2 %fusion.2 = f32[4,2,16,128]{3,0,2,1:T(4,128)S(1)} fusion(f32[2,64,16,4,128]{4,3,2,1,0:T(4,128)} %copy.171, f32[64,16,128]{2,1,0:T(8,128)S(1)} %fusion.87), kind=kLoop, calls=%fused_computation.6 | loop fusion | flops 2080768 | bytes 4784128 | tf_op jit(solution)/shard_map/reduce_sum | solution.py:70
  279.3 4.1 %collective-permute-done.36 = f32[8,16,128]{2,1,0:T(8,128)S(1)} collective-permute-done((f32[8,16,128]{2,1,0:T(8,128)S(1)}, f32[8,16,128]{2,1,0:T(8,128)S(1)}, u32[]{:S(2)}, u32[]{:S(2)}) %collective-permute-start.36) | collective-permute-done | bytes 65568 | tf_op jit(solution)/shard_map/ppermute | solution.py:19
  283.5 4.2 %collective-permute-start.39 = (f32[8,48,16]{2,1,0:T(8,128)S(1)}, f32[8,48,16]{2,1,0:T(8,128)S(1)}, u32[]{:S(2)}, u32[]{:S(2)}) collective-permute-start(f32[8,48,16]{2,1,0:T(8,128)S(1)} %get-tuple-element.41), channel_id=1, source_target_pairs={{1,0},{2,1},{3,2},{5,4},{6,5},{7,6},{9,8},{10,9},{11,10},{13,12},{... | collective-permute-start | bytes 73736 | tf_op jit(solution)/shard_map/ppermute | solution.py:22
  291.4 3.9 %collective-permute-done.38 = f32[8,48,16]{2,1,0:T(8,128)S(1)} collective-permute-done((f32[8,48,16]{2,1,0:T(8,128)S(1)}, f32[8,48,16]{2,1,0:T(8,128)S(1)}, u32[]{:S(2)}, u32[]{:S(2)}) %collective-permute-start.38) | collective-permute-done | bytes 24608 | tf_op jit(solution)/shard_map/ppermute | solution.py:19
  (154 shorter events, 130.4 us)
Async XLA Ops:
  1.7 24.5 %collective-permute-start = (f32[64,1,128]{2,1,0:T(1,128)S(1)}, f32[64,1,128]{2,1,0:T(1,128)S(1)}, u32[]{:S(2)}, u32[]{:S(2)}) collective-permute-start(f32[64,1,128]{2,1,0:T(1,128)S(1)} %get-tuple-element.39), channel_id=1, source_target_pairs={{4,0},{8,4},{12,8},{16,12},{20,16},{24,20},{28,24},{5,1},{9,5},{13... | collective-permute-start | bytes 98312 | tf_op jit(solution)/shard_map/ppermute | solution.py:22
  4.5 21.8 %collective-permute-start.1 = (f32[64,1,128]{2,1,0:T(1,128)S(1)}, f32[64,1,128]{2,1,0:T(1,128)S(1)}, u32[]{:S(2)}, u32[]{:S(2)}) collective-permute-start(f32[64,1,128]{2,1,0:T(1,128)S(1)} %get-tuple-element.38), channel_id=1, source_target_pairs={{0,4},{4,8},{8,12},{12,16},{16,20},{20,24},{24,28},{1,5},{5,9},{9,... | collective-permute-start | bytes 98312 | tf_op jit(solution)/shard_map/ppermute | solution.py:19
  21.0 127.2 %all-to-all-start = ((bf16[4,2,131072]{2,1,0:T(2,128)(2,1)}), bf16[4,2,131072]{2,1,0:T(2,128)(2,1)S(1)}, u32[]{:S(2)}, u32[]{:S(2)}) async-start(bf16[4,2,131072]{2,1,0:T(2,128)(2,1)} %reshape.19), calls=%async_computation | async-start | bytes 4194304 | tf_op jit(solution)/shard_map/all_to_all | solution.py:66
  29.0 44.2 %collective-permute-start.3 = (f32[64,18,1]{0,1,2:T(8,128)S(1)}, f32[64,18,1]{0,1,2:T(8,128)S(1)}, u32[]{:S(2)}, u32[]{:S(2)}) collective-permute-start(f32[64,18,1]{0,1,2:T(8,128)S(1)} %copy.174), channel_id=1, source_target_pairs={{0,1},{1,2},{2,3},{4,5},{5,6},{6,7},{8,9},{9,10},{10,11},{12,13},{... | collective-permute-start | bytes 13832 | tf_op jit(solution)/shard_map/ppermute | solution.py:19
  32.7 40.9 %collective-permute-start.2 = (f32[64,18,1]{0,1,2:T(8,128)S(1)}, f32[64,18,1]{0,1,2:T(8,128)S(1)}, u32[]{:S(2)}, u32[]{:S(2)}) collective-permute-start(f32[64,18,1]{0,1,2:T(8,128)S(1)} %copy.172), channel_id=1, source_target_pairs={{1,0},{2,1},{3,2},{5,4},{6,5},{7,6},{9,8},{10,9},{11,10},{13,12},{... | collective-permute-start | bytes 13832 | tf_op jit(solution)/shard_map/ppermute | solution.py:22
  79.8 6.1 %collective-permute-start.5 = (f32[64,1,128]{2,1,0:T(1,128)S(1)}, f32[64,1,128]{2,1,0:T(1,128)S(1)}, u32[]{:S(2)}, u32[]{:S(2)}) collective-permute-start(f32[64,1,128]{2,1,0:T(1,128)S(1)} %get-tuple-element.36), channel_id=1, source_target_pairs={{0,4},{4,8},{8,12},{12,16},{16,20},{20,24},{24,28},{1,5},{5,9},{9,... | collective-permute-start | bytes 98312 | tf_op jit(solution)/shard_map/ppermute | solution.py:19
  88.6 6.2 %collective-permute-start.7 = (f32[64,18,1]{0,1,2:T(8,128)S(1)}, f32[64,18,1]{0,1,2:T(8,128)S(1)}, u32[]{:S(2)}, u32[]{:S(2)}) collective-permute-start(f32[64,18,1]{0,1,2:T(8,128)S(1)} %copy.178), channel_id=1, source_target_pairs={{0,1},{1,2},{2,3},{4,5},{5,6},{6,7},{8,9},{9,10},{10,11},{12,13},{... | collective-permute-start | bytes 13832 | tf_op jit(solution)/shard_map/ppermute | solution.py:19
  90.9 5.6 %collective-permute-start.6 = (f32[64,18,1]{0,1,2:T(8,128)S(1)}, f32[64,18,1]{0,1,2:T(8,128)S(1)}, u32[]{:S(2)}, u32[]{:S(2)}) collective-permute-start(f32[64,18,1]{0,1,2:T(8,128)S(1)} %copy.176), channel_id=1, source_target_pairs={{1,0},{2,1},{3,2},{5,4},{6,5},{7,6},{9,8},{10,9},{11,10},{13,12},{... | collective-permute-start | bytes 13832 | tf_op jit(solution)/shard_map/ppermute | solution.py:22
  103.0 6.1 %collective-permute-start.9 = (f32[64,1,128]{2,1,0:T(1,128)S(1)}, f32[64,1,128]{2,1,0:T(1,128)S(1)}, u32[]{:S(2)}, u32[]{:S(2)}) collective-permute-start(f32[64,1,128]{2,1,0:T(1,128)S(1)} %get-tuple-element.34), channel_id=1, source_target_pairs={{0,4},{4,8},{8,12},{12,16},{16,20},{20,24},{24,28},{1,5},{5,9},{9,... | collective-permute-start | bytes 98312 | tf_op jit(solution)/shard_map/ppermute | solution.py:19
  112.1 7.3 %collective-permute-start.11 = (f32[64,18,1]{0,1,2:T(8,128)S(1)}, f32[64,18,1]{0,1,2:T(8,128)S(1)}, u32[]{:S(2)}, u32[]{:S(2)}) collective-permute-start(f32[64,18,1]{0,1,2:T(8,128)S(1)} %copy.182), channel_id=1, source_target_pairs={{0,1},{1,2},{2,3},{4,5},{5,6},{6,7},{8,9},{9,10},{10,11},{12,13},{... | collective-permute-start | bytes 13832 | tf_op jit(solution)/shard_map/ppermute | solution.py:19
  115.4 5.6 %collective-permute-start.10 = (f32[64,18,1]{0,1,2:T(8,128)S(1)}, f32[64,18,1]{0,1,2:T(8,128)S(1)}, u32[]{:S(2)}, u32[]{:S(2)}) collective-permute-start(f32[64,18,1]{0,1,2:T(8,128)S(1)} %copy.180), channel_id=1, source_target_pairs={{1,0},{2,1},{3,2},{5,4},{6,5},{7,6},{9,8},{10,9},{11,10},{13,12},{... | collective-permute-start | bytes 13832 | tf_op jit(solution)/shard_map/ppermute | solution.py:22
  126.4 6.1 %collective-permute-start.13 = (f32[64,1,128]{2,1,0:T(1,128)S(1)}, f32[64,1,128]{2,1,0:T(1,128)S(1)}, u32[]{:S(2)}, u32[]{:S(2)}) collective-permute-start(f32[64,1,128]{2,1,0:T(1,128)S(1)} %get-tuple-element.32), channel_id=1, source_target_pairs={{0,4},{4,8},{8,12},{12,16},{16,20},{20,24},{24,28},{1,5},{5,9},{9,... | collective-permute-start | bytes 98312 | tf_op jit(solution)/shard_map/ppermute | solution.py:19
  135.2 6.3 %collective-permute-start.15 = (f32[64,18,1]{0,1,2:T(8,128)S(1)}, f32[64,18,1]{0,1,2:T(8,128)S(1)}, u32[]{:S(2)}, u32[]{:S(2)}) collective-permute-start(f32[64,18,1]{0,1,2:T(8,128)S(1)} %copy.186), channel_id=1, source_target_pairs={{0,1},{1,2},{2,3},{4,5},{5,6},{6,7},{8,9},{9,10},{10,11},{12,13},{... | collective-permute-start | bytes 13832 | tf_op jit(solution)/shard_map/ppermute | solution.py:19
  137.5 5.6 %collective-permute-start.14 = (f32[64,18,1]{0,1,2:T(8,128)S(1)}, f32[64,18,1]{0,1,2:T(8,128)S(1)}, u32[]{:S(2)}, u32[]{:S(2)}) collective-permute-start(f32[64,18,1]{0,1,2:T(8,128)S(1)} %copy.184), channel_id=1, source_target_pairs={{1,0},{2,1},{3,2},{5,4},{6,5},{7,6},{9,8},{10,9},{11,10},{13,12},{... | collective-permute-start | bytes 13832 | tf_op jit(solution)/shard_map/ppermute | solution.py:22
  164.8 6.5 %collective-permute-start.16 = (f32[8,16,128]{2,1,0:T(8,128)S(1)}, f32[8,16,128]{2,1,0:T(8,128)S(1)}, u32[]{:S(2)}, u32[]{:S(2)}) collective-permute-start(f32[8,16,128]{2,1,0:T(8,128)S(1)} %bitcast.24), channel_id=1, source_target_pairs={{0,4},{4,8},{8,12},{12,16},{16,20},{20,24},{24,28},{1,5},{5,9},{9,... | collective-permute-start | bytes 196616 | tf_op jit(solution)/shard_map/ppermute | solution.py:19
  171.4 7.8 %collective-permute-start.19 = (f32[8,48,16]{2,1,0:T(8,128)S(1)}, f32[8,48,16]{2,1,0:T(8,128)S(1)}, u32[]{:S(2)}, u32[]{:S(2)}) collective-permute-start(f32[8,48,16]{2,1,0:T(8,128)S(1)} %get-tuple-element.43), channel_id=1, source_target_pairs={{1,0},{2,1},{3,2},{5,4},{6,5},{7,6},{9,8},{10,9},{11,10},{13,12},{... | collective-permute-start | bytes 73736 | tf_op jit(solution)/shard_map/ppermute | solution.py:22
  175.6 7.6 %collective-permute-start.18 = (f32[8,48,16]{2,1,0:T(8,128)S(1)}, f32[8,48,16]{2,1,0:T(8,128)S(1)}, u32[]{:S(2)}, u32[]{:S(2)}) collective-permute-start(f32[8,48,16]{2,1,0:T(8,128)S(1)} %get-tuple-element.42), channel_id=1, source_target_pairs={{0,1},{1,2},{2,3},{4,5},{5,6},{6,7},{8,9},{9,10},{10,11},{12,13},{... | collective-permute-start | bytes 73736 | tf_op jit(solution)/shard_map/ppermute | solution.py:19
  188.6 6.1 %collective-permute-start.21 = (f32[64,1,128]{2,1,0:T(1,128)S(1)}, f32[64,1,128]{2,1,0:T(1,128)S(1)}, u32[]{:S(2)}, u32[]{:S(2)}) collective-permute-start(f32[64,1,128]{2,1,0:T(1,128)S(1)} %get-tuple-element.30), channel_id=1, source_target_pairs={{0,4},{4,8},{8,12},{12,16},{16,20},{20,24},{24,28},{1,5},{5,9},{9,... | collective-permute-start | bytes 98312 | tf_op jit(solution)/shard_map/ppermute | solution.py:19
  195.5 6.2 %collective-permute-start.23 = (f32[64,18,1]{0,1,2:T(8,128)S(1)}, f32[64,18,1]{0,1,2:T(8,128)S(1)}, u32[]{:S(2)}, u32[]{:S(2)}) collective-permute-start(f32[64,18,1]{0,1,2:T(8,128)S(1)} %copy.192), channel_id=1, source_target_pairs={{0,1},{1,2},{2,3},{4,5},{5,6},{6,7},{8,9},{9,10},{10,11},{12,13},{... | collective-permute-start | bytes 13832 | tf_op jit(solution)/shard_map/ppermute | solution.py:19
  197.7 5.6 %collective-permute-start.22 = (f32[64,18,1]{0,1,2:T(8,128)S(1)}, f32[64,18,1]{0,1,2:T(8,128)S(1)}, u32[]{:S(2)}, u32[]{:S(2)}) collective-permute-start(f32[64,18,1]{0,1,2:T(8,128)S(1)} %copy.190), channel_id=1, source_target_pairs={{1,0},{2,1},{3,2},{5,4},{6,5},{7,6},{9,8},{10,9},{11,10},{13,12},{... | collective-permute-start | bytes 13832 | tf_op jit(solution)/shard_map/ppermute | solution.py:22
  208.4 6.1 %collective-permute-start.25 = (f32[64,1,128]{2,1,0:T(1,128)S(1)}, f32[64,1,128]{2,1,0:T(1,128)S(1)}, u32[]{:S(2)}, u32[]{:S(2)}) collective-permute-start(f32[64,1,128]{2,1,0:T(1,128)S(1)} %get-tuple-element.28), channel_id=1, source_target_pairs={{0,4},{4,8},{8,12},{12,16},{16,20},{20,24},{24,28},{1,5},{5,9},{9,... | collective-permute-start | bytes 98312 | tf_op jit(solution)/shard_map/ppermute | solution.py:19
  217.3 6.4 %collective-permute-start.27 = (f32[64,18,1]{0,1,2:T(8,128)S(1)}, f32[64,18,1]{0,1,2:T(8,128)S(1)}, u32[]{:S(2)}, u32[]{:S(2)}) collective-permute-start(f32[64,18,1]{0,1,2:T(8,128)S(1)} %copy.196), channel_id=1, source_target_pairs={{0,1},{1,2},{2,3},{4,5},{5,6},{6,7},{8,9},{9,10},{10,11},{12,13},{... | collective-permute-start | bytes 13832 | tf_op jit(solution)/shard_map/ppermute | solution.py:19
  219.5 5.6 %collective-permute-start.26 = (f32[64,18,1]{0,1,2:T(8,128)S(1)}, f32[64,18,1]{0,1,2:T(8,128)S(1)}, u32[]{:S(2)}, u32[]{:S(2)}) collective-permute-start(f32[64,18,1]{0,1,2:T(8,128)S(1)} %copy.194), channel_id=1, source_target_pairs={{1,0},{2,1},{3,2},{5,4},{6,5},{7,6},{9,8},{10,9},{11,10},{13,12},{... | collective-permute-start | bytes 13832 | tf_op jit(solution)/shard_map/ppermute | solution.py:22
  230.2 6.1 %collective-permute-start.29 = (f32[64,1,128]{2,1,0:T(1,128)S(1)}, f32[64,1,128]{2,1,0:T(1,128)S(1)}, u32[]{:S(2)}, u32[]{:S(2)}) collective-permute-start(f32[64,1,128]{2,1,0:T(1,128)S(1)} %get-tuple-element.26), channel_id=1, source_target_pairs={{0,4},{4,8},{8,12},{12,16},{16,20},{20,24},{24,28},{1,5},{5,9},{9,... | collective-permute-start | bytes 98312 | tf_op jit(solution)/shard_map/ppermute | solution.py:19
  239.0 6.2 %collective-permute-start.31 = (f32[64,18,1]{0,1,2:T(8,128)S(1)}, f32[64,18,1]{0,1,2:T(8,128)S(1)}, u32[]{:S(2)}, u32[]{:S(2)}) collective-permute-start(f32[64,18,1]{0,1,2:T(8,128)S(1)} %copy.200), channel_id=1, source_target_pairs={{0,1},{1,2},{2,3},{4,5},{5,6},{6,7},{8,9},{9,10},{10,11},{12,13},{... | collective-permute-start | bytes 13832 | tf_op jit(solution)/shard_map/ppermute | solution.py:19
  241.3 5.6 %collective-permute-start.30 = (f32[64,18,1]{0,1,2:T(8,128)S(1)}, f32[64,18,1]{0,1,2:T(8,128)S(1)}, u32[]{:S(2)}, u32[]{:S(2)}) collective-permute-start(f32[64,18,1]{0,1,2:T(8,128)S(1)} %copy.198), channel_id=1, source_target_pairs={{1,0},{2,1},{3,2},{5,4},{6,5},{7,6},{9,8},{10,9},{11,10},{13,12},{... | collective-permute-start | bytes 13832 | tf_op jit(solution)/shard_map/ppermute | solution.py:22
  252.0 6.1 %collective-permute-start.33 = (f32[64,1,128]{2,1,0:T(1,128)S(1)}, f32[64,1,128]{2,1,0:T(1,128)S(1)}, u32[]{:S(2)}, u32[]{:S(2)}) collective-permute-start(f32[64,1,128]{2,1,0:T(1,128)S(1)} %get-tuple-element.24), channel_id=1, source_target_pairs={{0,4},{4,8},{8,12},{12,16},{16,20},{20,24},{24,28},{1,5},{5,9},{9,... | collective-permute-start | bytes 98312 | tf_op jit(solution)/shard_map/ppermute | solution.py:19
  260.8 6.2 %collective-permute-start.35 = (f32[64,18,1]{0,1,2:T(8,128)S(1)}, f32[64,18,1]{0,1,2:T(8,128)S(1)}, u32[]{:S(2)}, u32[]{:S(2)}) collective-permute-start(f32[64,18,1]{0,1,2:T(8,128)S(1)} %copy.204), channel_id=1, source_target_pairs={{0,1},{1,2},{2,3},{4,5},{5,6},{6,7},{8,9},{9,10},{10,11},{12,13},{... | collective-permute-start | bytes 13832 | tf_op jit(solution)/shard_map/ppermute | solution.py:19
  263.1 5.6 %collective-permute-start.34 = (f32[64,18,1]{0,1,2:T(8,128)S(1)}, f32[64,18,1]{0,1,2:T(8,128)S(1)}, u32[]{:S(2)}, u32[]{:S(2)}) collective-permute-start(f32[64,18,1]{0,1,2:T(8,128)S(1)} %copy.202), channel_id=1, source_target_pairs={{1,0},{2,1},{3,2},{5,4},{6,5},{7,6},{9,8},{10,9},{11,10},{13,12},{... | collective-permute-start | bytes 13832 | tf_op jit(solution)/shard_map/ppermute | solution.py:22
  276.9 6.5 %collective-permute-start.36 = (f32[8,16,128]{2,1,0:T(8,128)S(1)}, f32[8,16,128]{2,1,0:T(8,128)S(1)}, u32[]{:S(2)}, u32[]{:S(2)}) collective-permute-start(f32[8,16,128]{2,1,0:T(8,128)S(1)} %bitcast.28), channel_id=1, source_target_pairs={{0,4},{4,8},{8,12},{12,16},{16,20},{20,24},{24,28},{1,5},{5,9},{9,... | collective-permute-start | bytes 196616 | tf_op jit(solution)/shard_map/ppermute | solution.py:19
  283.5 7.8 %collective-permute-start.39 = (f32[8,48,16]{2,1,0:T(8,128)S(1)}, f32[8,48,16]{2,1,0:T(8,128)S(1)}, u32[]{:S(2)}, u32[]{:S(2)}) collective-permute-start(f32[8,48,16]{2,1,0:T(8,128)S(1)} %get-tuple-element.41), channel_id=1, source_target_pairs={{1,0},{2,1},{3,2},{5,4},{6,5},{7,6},{9,8},{10,9},{11,10},{13,12},{... | collective-permute-start | bytes 73736 | tf_op jit(solution)/shard_map/ppermute | solution.py:22
  287.7 7.6 %collective-permute-start.38 = (f32[8,48,16]{2,1,0:T(8,128)S(1)}, f32[8,48,16]{2,1,0:T(8,128)S(1)}, u32[]{:S(2)}, u32[]{:S(2)}) collective-permute-start(f32[8,48,16]{2,1,0:T(8,128)S(1)} %get-tuple-element.40), channel_id=1, source_target_pairs={{0,1},{1,2},{2,3},{4,5},{5,6},{6,7},{8,9},{9,10},{10,11},{12,13},{... | collective-permute-start | bytes 73736 | tf_op jit(solution)/shard_map/ppermute | solution.py:19
  (17 other events, 201.8 us)
where the time goes:
time: 303 us; the launch traced here: 300 us
  starting transfers between devices  109 us (36%)
  waiting for transfers between devices  90.8 us (30%)
  local copies, waits for them, and re-layouts  64.7 us (21%)
  other arithmetic  34 us (11%)
    ppermute x20, waiting for transfers between devices, padded_2(): lax.ppermute(lax.slice_in_dim(block, block.shape[dim] - width, None, axis...  80.5 us
    ppermute x20, starting transfers between devices, padded_2(): lax.ppermute(lax.slice_in_dim(block, 0, width, axis=dim), axis, backward)  59.8 us
    ppermute x20, starting transfers between devices, padded_2(): lax.ppermute(lax.slice_in_dim(block, block.shape[dim] - width, None, axis...  43.8 us
    unnamed x19, local copies, waits for them, and re-layouts  18.7 us
    sub x6, other arithmetic, advance(): return result - wind_y[:, None, None] * (center - ahead_y)  13.1 us
    slice x16, local copies, waits for them, and re-layouts, padded_2(): lax.slice_in_dim(block, 0, width, axis=dim)  12.3 us
    slice x18, local copies, waits for them, and re-layouts, padded_2(): lax.slice_in_dim(block, block.shape[dim] - width, None, axis=dim)  11.9 us
    ppermute x20, waiting for transfers between devices, padded_2(): lax.ppermute(lax.slice_in_dim(block, 0, width, axis=dim), axis, backward)  10.3 us
  transfers between devices with their start and end apart: 41, of which 21 were waited for; matrix products, arithmetic and copies ran while one was open for 17% of the time, Pallas kernels for 0%

commit v1 on v0

v1 whole, which is shorter than its diff:
```python
import functools

import jax
import jax.numpy as jnp
from jax import lax
from jax.experimental import pallas as pl
from jax.experimental.pallas import tpu as pltpu
from jax.sharding import PartitionSpec as P

ITERS = 2
MODEL_STEPS = 4
DIFFUSION = 0.1
RELAX = 0.5
REACH = 16
TAPER_TOTAL = sum(1.0 - (k / 17.0) ** 2 for k in range(-REACH, REACH + 1))
F32 = jnp.float32
BF16 = jnp.bfloat16
LANES = 128
SUB = 8

VMEM = pl.BlockSpec(memory_space=pltpu.VMEM)
SMEM = pl.BlockSpec(memory_space=pltpu.SMEM)
PARAMS = pltpu.CompilerParams(vmem_limit_bytes=48 * 1024 * 1024)


def call(body, out_shape, *args, in_specs=None, scratch=()):
    return pl.pallas_call(
        body,
        out_shape=out_shape,
        in_specs=in_specs or [VMEM] * len(args),
        out_specs=jax.tree.map(lambda _: VMEM, out_shape),
        scratch_shapes=scratch,
        compiler_params=PARAMS,
    )(*args)


def lane_iota(shape):
    return lax.broadcasted_iota(jnp.int32, shape, len(shape) - 1)


def sub_iota(shape):
    return lax.broadcasted_iota(jnp.int32, shape, len(shape) - 2)


def split_body(in_ref, out_ref):
    out_ref[0] = in_ref[...]


def split_columns(members, parts):
    own, levels, rows, ny = members.shape
    cols = ny // parts
    return pl.pallas_call(
        split_body,
        out_shape=jax.ShapeDtypeStruct((parts, own, levels, rows, cols), members.dtype),
        grid=(parts,),
        in_specs=[pl.BlockSpec((own, levels, rows, cols), lambda c: (0, 0, 0, c))],
        out_specs=pl.BlockSpec((1, own, levels, rows, cols), lambda c: (c, 0, 0, 0, 0)),
        compiler_params=PARAMS,
    )(members)


def edge_body(x_ref, first_ref, last_ref):
    levels, rows, cols = x_ref.shape
    group = LANES // MODEL_STEPS
    slot = lane_iota((rows, LANES)) // MODEL_STEPS
    for g in range(levels // group):
        first = jnp.zeros((rows, LANES), F32)
        last = jnp.zeros((rows, LANES), F32)
        for k in range(group):
            x = x_ref[g * group + k]
            here = slot == k
            first = jnp.where(here, pltpu.roll(x, (MODEL_STEPS * k) % LANES, 1), first)
            last = jnp.where(here, pltpu.roll(x, (MODEL_STEPS * (k + 1)) % LANES, 1), last)
        first_ref[g] = first
        last_ref[g] = last


def edge_columns(x):
    levels, rows, cols = x.shape
    out = jax.ShapeDtypeStruct((levels * MODEL_STEPS // LANES, rows, LANES), F32)
    return call(edge_body, (out, out), x)


def rows_body(x_ref, left_ref, right_ref, top_ref, bottom_ref):
    upper = sub_iota((SUB, LANES)) < MODEL_STEPS
    at = 0
    for ref in (x_ref, left_ref, right_ref):
        count, rows, _ = ref.shape
        for q in range(count // 2):
            top_ref[at] = jnp.where(upper, ref[2 * q, :SUB], pltpu.roll(ref[2 * q + 1, :SUB], MODEL_STEPS, 0))
            bottom_ref[at] = jnp.where(
                upper, pltpu.roll(ref[2 * q, rows - SUB :], MODEL_STEPS, 0), ref[2 * q + 1, rows - SUB :]
            )
            at += 1


def edge_rows(x, left, right):
    count = (x.shape[0] + left.shape[0] + right.shape[0]) // 2
    out = jax.ShapeDtypeStruct((count, SUB, LANES), F32)
    return call(rows_body, (out, out), x, left, right)


def shift(x, axis, step):
    count = lax.axis_size(axis)
    pairs = [(i, i + step) for i in range(count) if 0 <= i + step < count]
    return lax.ppermute(x, axis, pairs)


def halo_of(x):
    first, last = edge_columns(x)
    left = shift(last, "member", 1)
    right = shift(first, "member", -1)
    return left, right


def halo_rows_of(x, left, right):
    top, bottom = edge_rows(x, left, right)
    above = shift(bottom, "tile", 1)
    below = shift(top, "tile", -1)
    return above, below


def third_tile(below, above, odd):
    upper = sub_iota((SUB, LANES)) < MODEL_STEPS
    if odd:
        return jnp.where(upper, pltpu.roll(below, MODEL_STEPS, 0), above)
    return jnp.where(upper, below, pltpu.roll(above, MODEL_STEPS, 0))


def sweep_block(level_pair, x_ref, sides, above_ref, below_ref, wx_ref, wy_ref, mask, emit):
    lanes = lane_iota((x_ref.shape[1] + SUB, LANES))
    group = LANES // MODEL_STEPS
    rows = x_ref.shape[1]
    ext_rows = rows + SUB
    ext_cols = 2 * LANES
    above = above_ref[level_pair]
    below = below_ref[level_pair]
    for odd in range(2):
        level = 2 * level_pair + odd
        g = level // group
        k = level % group
        left = sides[0][g]
        right = sides[1][g]
        at = (LANES - MODEL_STEPS * k) % LANES
        side_right = pltpu.roll(right, at, 1)
        side_left = pltpu.roll(left, (at + LANES - MODEL_STEPS) % LANES, 1)
        side = jnp.where(lanes < MODEL_STEPS, side_right, side_left)
        center = jnp.concatenate([x_ref[level], third_tile(below, above, odd)], axis=0)
        field = jnp.concatenate([center, side], axis=1) * mask
        wx = wx_ref[level]
        wy = wy_ref[level]
        own = 1.0 - 4.0 * DIFFUSION - wx - wy
        ahead_x = DIFFUSION + wx
        ahead_y = DIFFUSION + wy
        for _ in range(MODEL_STEPS):
            field = (
                own * field
                + ahead_x * pltpu.roll(field, ext_rows - 1, 0)
                + ahead_y * pltpu.roll(field, ext_cols - 1, 1)
                + DIFFUSION * (pltpu.roll(field, 1, 0) + pltpu.roll(field, 1, 1))
            ) * mask
        emit(level, field[:rows, :LANES])


def block_mask(place_ref, rows, cols):
    tile, tiles, member, parts = (place_ref[i] for i in range(4))
    shape = (rows + SUB, 2 * LANES)
    r = sub_iota(shape)
    c = lane_iota(shape)
    r = jnp.where(r < rows + MODEL_STEPS, r, r - rows - SUB)
    near = (c < cols + MODEL_STEPS) | (c >= 2 * LANES - MODEL_STEPS)
    c = jnp.where(c < cols + MODEL_STEPS, c, c - 2 * LANES)
    gr = r + tile * rows
    gc = c + member * cols
    inside = (gr >= 0) & (gr < tiles * rows) & (gc >= 0) & (gc < parts * cols) & near
    return jnp.where(inside, 1.0, 0.0).astype(F32)


def make_sides(left_ref, right_ref, above_ref, below_ref, levels, sides_ref):
    groups, rows, _ = left_ref.shape
    for s, ref in enumerate((left_ref, right_ref)):
        for g in range(groups):
            at = (levels + s * groups + g) // 2
            sides_ref[s, g, :rows] = ref[g]
            sides_ref[s, g, rows:] = third_tile(below_ref[at], above_ref[at], g % 2)


def model_body(place_ref, wx_ref, wy_ref, x_ref, left_ref, right_ref, above_ref, below_ref, grad_ref, sides_ref):
    levels, rows, cols = x_ref.shape
    mask = block_mask(place_ref, rows, cols)
    make_sides(left_ref, right_ref, above_ref, below_ref, levels, sides_ref)
    sides = (sides_ref.at[0], sides_ref.at[1])

    def emit(level, value):
        grad_ref[level] = value

    def step(q, carry):
        for u in range(2):
            sweep_block(2 * q + u, x_ref, sides, above_ref, below_ref, wx_ref, wy_ref, mask, emit)
        return carry

    lax.fori_loop(0, levels // 4, step, 0)


def model(place, wind_x, wind_y, x, left, right, above, below):
    levels, rows, cols = x.shape
    groups = left.shape[0]
    return call(
        model_body,
        jax.ShapeDtypeStruct(x.shape, F32),
        place, wind_x, wind_y, x, left, right, above, below,
        in_specs=[SMEM] * 3 + [VMEM] * 5,
        scratch=[pltpu.VMEM((2, groups, rows + SUB, LANES), F32)],
    )


def project_body(members_ref, grad_ref, out_ref):
    parts, own, levels, rows, cols = members_ref.shape
    count = parts * own

    def step(q, carry):
        carry = list(carry)
        for u in range(2):
            level = 2 * q + u
            g = grad_ref[level]
            for m in range(count):
                carry[m] = carry[m] + members_ref[m // own, m % own, level].astype(F32) * g
        return tuple(carry)

    zero = jnp.zeros((rows, cols), F32)
    total = lax.fori_loop(0, levels // 2, step, (zero,) * count)
    for m in range(count):
        out_ref[m] = total[m].astype(out_ref.dtype)


def project(members, grad, dtype):
    parts, own, levels, rows, cols = members.shape
    return call(project_body, jax.ShapeDtypeStruct((parts * own, rows, cols), dtype), members, grad)


def taper(offset):
    k = offset.astype(F32)
    w = (1.0 - (k / 17.0) * (k / 17.0)) * (1.0 / TAPER_TOTAL)
    return jnp.where(jnp.abs(offset) <= REACH, w, 0.0)


def halves(x):
    high = x.astype(BF16)
    return high, (x - high.astype(F32)).astype(BF16)


def sharp_dot(a, b):
    ah, al = halves(a)
    bh, bl = halves(b)
    dot = functools.partial(jnp.dot, preferred_element_type=F32)
    return dot(ah, bh) + dot(al, bh) + dot(ah, bl)


def smooth_columns(wide, cols):
    shape = (3 * cols, cols)
    band = taper(sub_iota(shape) - lane_iota(shape) - cols)
    return sharp_dot(wide, band)


def smooth_rows(tall, rows):
    shape = (rows, 3 * rows)
    band = taper(lane_iota(shape) - sub_iota(shape) - rows)
    return sharp_dot(band, tall)


def columns_body(left_ref, mid_ref, right_ref, out_ref):
    count, rows, cols = mid_ref.shape
    wide = jnp.concatenate([r[...].reshape(count * rows, cols).astype(F32) for r in (left_ref, mid_ref, right_ref)], axis=1)
    out_ref[...] = smooth_columns(wide, cols).reshape(count, rows, cols)


def increments(members_ref, local_ref, emit):
    parts, own, levels, rows, cols = members_ref.shape
    local = [local_ref[m] for m in range(parts * own)]

    def step(q, carry):
        for u in range(2):
            level = 2 * q + u
            total = members_ref[0, 0, level].astype(F32) * local[0]
            for m in range(1, parts * own):
                total = total + members_ref[m // own, m % own, level].astype(F32) * local[m]
            emit(level, total)
        return carry

    lax.fori_loop(0, levels // 2, step, 0)


def update_body(members_ref, residual_ref, above_ref, mid_ref, below_ref, analysis_ref, out_ref, local_ref):
    count, rows, cols = mid_ref.shape
    for m in range(count):
        local_ref[m] = smooth_rows(jnp.concatenate([above_ref[m], mid_ref[m], below_ref[m]], axis=0), rows)

    def emit(level, value):
        analysis_ref[level] = value
        out_ref[level] = residual_ref[level] - RELAX * value

    increments(members_ref, local_ref, emit)


def final_body(place_ref, members_ref, residual_ref, before_ref, all_ref, analysis_ref, out_ref, local_ref, wide_ref):
    _, count, rows, cols = all_ref.shape
    tile, tiles, member, parts = (place_ref[i] for i in range(4))
    for i in range(3):
        for j in range(3):
            t = tile + i - 1
            c = member + j - 1
            ok = (t >= 0) & (t < tiles) & (c >= 0) & (c < parts)
            at = jnp.clip(t, 0, tiles - 1) * parts + jnp.clip(c, 0, parts - 1)
            block = all_ref[at].astype(F32) * jnp.where(ok, 1.0, 0.0)
            wide_ref[:, i * rows : (i + 1) * rows, j * cols : (j + 1) * cols] = block
    wide = wide_ref[...].reshape(count * 3 * rows, 3 * cols)
    tall = smooth_columns(wide, cols).reshape(count, 3 * rows, cols)
    for m in range(count):
        local_ref[m] = smooth_rows(tall[m], rows)

    def emit(level, value):
        analysis_ref[level] = before_ref[level] + value
        out_ref[level] = residual_ref[level] - RELAX * value

    increments(members_ref, local_ref, emit)


def per_device(residual_in, members, wind_x, wind_y):
    levels, rows, cols = residual_in.shape
    tiles = lax.axis_size("tile")
    parts = lax.axis_size("member")
    place = jnp.stack([lax.axis_index("tile"), jnp.int32(tiles), lax.axis_index("member"), jnp.int32(parts)])
    count = members.shape[0] * parts
    like = jax.ShapeDtypeStruct(residual_in.shape, F32)
    small = jax.ShapeDtypeStruct((count, rows, cols), F32)

    left, right = halo_of(residual_in)
    outgoing = split_columns(members, parts)
    block = lax.all_to_all(outgoing, "member", split_axis=0, concat_axis=0, tiled=True)
    above, below = halo_rows_of(residual_in, left, right)
    grad = model(place, wind_x, wind_y, residual_in, left, right, above, below)

    mid = project(block, grad, F32)
    smooth = call(columns_body, small, shift(mid, "member", 1), mid, shift(mid, "member", -1))
    analysis, residual = call(
        update_body, (like, like),
        block, residual_in, shift(smooth, "tile", 1), smooth, shift(smooth, "tile", -1),
        scratch=[pltpu.VMEM((count, rows, cols), F32)],
    )

    left, right = halo_of(residual)
    above, below = halo_rows_of(residual, left, right)
    grad = model(place, wind_x, wind_y, residual, left, right, above, below)
    mid = project(block, grad, BF16)
    everywhere = lax.all_gather(mid, ("tile", "member"), axis=0, tiled=False)
    return call(
        final_body, (like, like),
        place, block, residual, analysis, everywhere,
        in_specs=[SMEM] + [VMEM] * 4,
        scratch=[pltpu.VMEM((count, rows, cols), F32), pltpu.VMEM((count, 3 * rows, 3 * cols), F32)],
    )


def solution(mesh):
    return jax.shard_map(
        per_device,
        mesh=mesh,
        in_specs=(P(None, "tile", "member"), P("member", None, "tile", None), P(), P()),
        out_specs=(P(None, "tile", "member"), P(None, "tile", "member")),
        check_vma=False,
    )
```

time: 303 us -> 195 us (0.64)
  starting transfers between devices: 109 us -> 40.8 us
  local copies, waits for them, and re-layouts: 64.7 us -> 4.95 us
  other arithmetic: 34 us -> 0.08 us
  Pallas kernels: 0 us -> 22.5 us
  waiting for transfers between devices: 90.8 us -> 109 us
  between operations: 1.48 us -> 14.2 us
    ppermute x40 -> x12, starting transfers between devices: 104 us -> 35.5 us  [shift(): return lax.ppermute(x, axis, pairs)]
    all_gather x0 -> x1, waiting for transfers between devices: none -> 53.1 us  [per_device(): everywhere = lax.all_gather(mid, ('tile', 'member'), axis=0, tiled=False)]
    ppermute x40 -> x12, waiting for transfers between devices: 90.8 us -> 55.8 us  [shift(): return lax.ppermute(x, axis, pairs)]
    slice x34 -> x0, local copies, waits for them, and re-layouts: 24.2 us -> none  [the longest x16 12.3 us: padded_2(): lax.slice_in_dim(block, 0, width, axis=dim)]
    pallas_call x0 -> x12, Pallas kernels: none -> 22.5 us  [the longest x11 21.9 us: call(): pl.pallas_call(body, out_shape=out_shape, in_specs=in_specs or [VMEM] * l...]
    ppermute x16 -> x0, local copies, waits for them, and re-layouts: 14.4 us -> none  [the longest x8 9.81 us: padded_2(): lax.ppermute(lax.slice_in_dim(block, 0, width, axis=dim), axis, backward)]
    sub x8 -> x0, other arithmetic: 14.2 us -> none  [the longest x6 13.1 us: advance(): return result - wind_y[:, None, None] * (center - ahead_y)]
    unnamed x19 -> x16, local copies, waits for them, and re-layouts: 18.7 us -> 4.95 us
  transfers between devices with their start and end apart: 41 -> 14, of which waited for: 21 -> 10; matrix products, arithmetic and copies ran while one was open for 17% -> 0% of each run, Pallas kernels for 0% -> 4%
where the time goes in v1:
time: 195 us; the launch traced here: 192 us
  waiting for transfers between devices  109 us (56%)
  starting transfers between devices  40.8 us (21%)
  Pallas kernels  22.5 us (12%)
  between operations  14.2 us (7%)
  local copies, waits for them, and re-layouts  4.95 us (3%)
    ppermute x12, waiting for transfers between devices, shift(): return lax.ppermute(x, axis, pairs)  55.8 us
    all_gather x1, waiting for transfers between devices, per_device(): everywhere = lax.all_gather(mid, ('tile', 'member'), axis=0, tiled=False)  53.1 us
    ppermute x12, starting transfers between devices, shift(): return lax.ppermute(x, axis, pairs)  35.5 us
    pallas_call x11, Pallas kernels, call(): pl.pallas_call(body, out_shape=out_shape, in_specs=in_specs or [VMEM] * l...  21.9 us
    all_to_all x1, starting transfers between devices, per_device(): lax.all_to_all(outgoing, 'member', split_axis=0, concat_axis=0, tiled=True)  5.34 us
    unnamed x16, local copies, waits for them, and re-layouts  4.95 us
  transfers between devices with their start and end apart: 14, of which 10 were waited for; matrix products, arithmetic and copies ran while one was open for 0% of the time, Pallas kernels for 4%

profile of v1, /device:TPU:20, one launch (start us, length us, event | category | flops | bytes accessed | tf_op | source)
XLA Modules:
  0.0 191.6 jit_solution(5155084212695956142)
XLA Ops:
  7.2 1.6 copy-done.2
  8.8 0.6 shard_map.59
  9.4 1.3 copy-done
  10.7 5.3 %all-to-all-start = ((bf16[4,2,64,16,128]{4,3,2,1,0:T(8,128)(2,1)}), bf16[4,2,64,16,128]{4,3,2,1,0:T(8,128)(2,1)S(1)}, u32[]{:S(2)}, u32[]{:S(2)}) async-start(bf16[4,2,64,16,128]{4,3,2,1,0:T(8,128)(2,1)} %copy-done), calls=%async_computation | async-start | bytes 4194304 | tf_op jit(solution)/shard_map/all_to_all | solution.py:339
  16.4 3.4 %collective-permute-start = (f32[2,16,128]{2,1,0:T(8,128)S(1)}, f32[2,16,128]{2,1,0:T(8,128)S(1)}, u32[]{:S(2)}, u32[]{:S(2)}) collective-permute-start(f32[2,16,128]{2,1,0:T(8,128)S(1)} %get-tuple-element.12), channel_id=1, source_target_pairs={{0,1},{1,2},{2,3},{4,5},{5,6},{6,7},{8,9},{9,10},{10,11},{12,13},{... | collective-permute-start | bytes 49160 | tf_op jit(solution)/shard_map/ppermute | solution.py:106
  19.7 2.5 %collective-permute-start.1 = (f32[2,16,128]{2,1,0:T(8,128)S(1)}, f32[2,16,128]{2,1,0:T(8,128)S(1)}, u32[]{:S(2)}, u32[]{:S(2)}) collective-permute-start(f32[2,16,128]{2,1,0:T(8,128)S(1)} %get-tuple-element.13), channel_id=1, source_target_pairs={{1,0},{2,1},{3,2},{5,4},{6,5},{7,6},{9,8},{10,9},{11,10},{13,12},{... | collective-permute-start | bytes 49160 | tf_op jit(solution)/shard_map/ppermute | solution.py:106
  22.2 40.0 %collective-permute-done.left_ref = f32[2,16,128]{2,1,0:T(8,128)S(1)} collective-permute-done((f32[2,16,128]{2,1,0:T(8,128)S(1)}, f32[2,16,128]{2,1,0:T(8,128)S(1)}, u32[]{:S(2)}, u32[]{:S(2)}) %collective-permute-start) | collective-permute-done | bytes 16416 | tf_op jit(solution)/shard_map/ppermute | solution.py:106
  62.3 1.9 %collective-permute-start.2 = (f32[34,8,128]{2,1,0:T(8,128)S(1)}, f32[34,8,128]{2,1,0:T(8,128)S(1)}, u32[]{:S(2)}, u32[]{:S(2)}) collective-permute-start(f32[34,8,128]{2,1,0:T(8,128)S(1)} %get-tuple-element.14), channel_id=1, source_target_pairs={{0,4},{4,8},{8,12},{12,16},{16,20},{20,24},{24,28},{1,5},{5,9},{9,... | collective-permute-start | bytes 417800 | tf_op jit(solution)/shard_map/ppermute | solution.py:106
  64.2 4.5 %collective-permute-start.3 = (f32[34,8,128]{2,1,0:T(8,128)S(1)}, f32[34,8,128]{2,1,0:T(8,128)S(1)}, u32[]{:S(2)}, u32[]{:S(2)}) collective-permute-start(f32[34,8,128]{2,1,0:T(8,128)S(1)} %get-tuple-element.15), channel_id=1, source_target_pairs={{4,0},{8,4},{12,8},{16,12},{20,16},{24,20},{28,24},{5,1},{9,5},{13... | collective-permute-start | bytes 417800 | tf_op jit(solution)/shard_map/ppermute | solution.py:106
  68.8 0.7 collective-permute-done.2.above_ref
  69.5 1.8 collective-permute-done.3.below_ref
  71.3 7.8 %shard_map.62.grad_ref = f32[64,16,128]{2,1,0:T(8,128)S(1)} custom-call(s32[4]{0:T(128)S(1)} %pad_add_fusion.place_ref, f32[64]{0:T(128)S(1)} %copy-done.6, f32[64]{0:T(128)S(1)} %copy-done.7, f32[64,16,128]{2,1,0:T(8,128)S(1)} %copy-done.1, f32[2,16,128]{2,1,0:T(8,128)S(1)} %collective-permute-done.left_ref, ...), custom_call_target="tpu_custom_call" | custom-call | tf_op jit(solution)/shard_map/pallas_call | solution.py:27
  79.7 3.4 %collective-permute-start.5 = (f32[8,16,128]{2,1,0:T(8,128)S(1)}, f32[8,16,128]{2,1,0:T(8,128)S(1)}, u32[]{:S(2)}, u32[]{:S(2)}) collective-permute-start(f32[8,16,128]{2,1,0:T(8,128)S(1)} %shard_map.63.mid_ref), channel_id=1, source_target_pairs={{1,0},{2,1},{3,2},{5,4},{6,5},{7,6},{9,8},{10,9},{11,10},{13,12},{... | collective-permute-start | bytes 196616 | tf_op jit(solution)/shard_map/ppermute | solution.py:106
  83.0 2.5 %collective-permute-start.4 = (f32[8,16,128]{2,1,0:T(8,128)S(1)}, f32[8,16,128]{2,1,0:T(8,128)S(1)}, u32[]{:S(2)}, u32[]{:S(2)}) collective-permute-start(f32[8,16,128]{2,1,0:T(8,128)S(1)} %shard_map.63.mid_ref), channel_id=1, source_target_pairs={{0,1},{1,2},{2,3},{4,5},{5,6},{6,7},{8,9},{9,10},{10,11},{12,13},{... | collective-permute-start | bytes 196616 | tf_op jit(solution)/shard_map/ppermute | solution.py:106
  85.5 0.9 collective-permute-done.5.right_ref
  86.4 3.1 %collective-permute-done.4.left_ref = f32[8,16,128]{2,1,0:T(8,128)S(1)} collective-permute-done((f32[8,16,128]{2,1,0:T(8,128)S(1)}, f32[8,16,128]{2,1,0:T(8,128)S(1)}, u32[]{:S(2)}, u32[]{:S(2)}) %collective-permute-start.4) | collective-permute-done | bytes 65568 | tf_op jit(solution)/shard_map/ppermute | solution.py:106
  89.8 3.0 %collective-permute-start.7 = (f32[8,16,128]{2,1,0:T(8,128)S(1)}, f32[8,16,128]{2,1,0:T(8,128)S(1)}, u32[]{:S(2)}, u32[]{:S(2)}) collective-permute-start(f32[8,16,128]{2,1,0:T(8,128)S(1)} %shard_map.64.mid_ref), channel_id=1, source_target_pairs={{4,0},{8,4},{12,8},{16,12},{20,16},{24,20},{28,24},{5,1},{9,5},{13... | collective-permute-start | bytes 196616 | tf_op jit(solution)/shard_map/ppermute | solution.py:106
  92.7 1.9 %collective-permute-start.6 = (f32[8,16,128]{2,1,0:T(8,128)S(1)}, f32[8,16,128]{2,1,0:T(8,128)S(1)}, u32[]{:S(2)}, u32[]{:S(2)}) collective-permute-start(f32[8,16,128]{2,1,0:T(8,128)S(1)} %shard_map.64.mid_ref), channel_id=1, source_target_pairs={{0,4},{4,8},{8,12},{12,16},{16,20},{20,24},{24,28},{1,5},{5,9},{9,... | collective-permute-start | bytes 196616 | tf_op jit(solution)/shard_map/ppermute | solution.py:106
  94.7 4.5 %collective-permute-done.6.above_ref = f32[8,16,128]{2,1,0:T(8,128)S(1)} collective-permute-done((f32[8,16,128]{2,1,0:T(8,128)S(1)}, f32[8,16,128]{2,1,0:T(8,128)S(1)}, u32[]{:S(2)}, u32[]{:S(2)}) %collective-permute-start.6) | collective-permute-done | bytes 65568 | tf_op jit(solution)/shard_map/ppermute | solution.py:106
  99.2 0.9 shard_map.65
  100.1 0.8 copy-done.4
  101.2 2.5 %collective-permute-start.8 = (f32[2,16,128]{2,1,0:T(8,128)S(1)}, f32[2,16,128]{2,1,0:T(8,128)S(1)}, u32[]{:S(2)}, u32[]{:S(2)}) collective-permute-start(f32[2,16,128]{2,1,0:T(8,128)S(1)} %get-tuple-element.18), channel_id=1, source_target_pairs={{0,1},{1,2},{2,3},{4,5},{5,6},{6,7},{8,9},{9,10},{10,11},{12,13},{... | collective-permute-start | bytes 49160 | tf_op jit(solution)/shard_map/ppermute | solution.py:106
  103.7 3.4 %collective-permute-start.9 = (f32[2,16,128]{2,1,0:T(8,128)S(1)}, f32[2,16,128]{2,1,0:T(8,128)S(1)}, u32[]{:S(2)}, u32[]{:S(2)}) collective-permute-start(f32[2,16,128]{2,1,0:T(8,128)S(1)} %get-tuple-element.19), channel_id=1, source_target_pairs={{1,0},{2,1},{3,2},{5,4},{6,5},{7,6},{9,8},{10,9},{11,10},{13,12},{... | collective-permute-start | bytes 49160 | tf_op jit(solution)/shard_map/ppermute | solution.py:106
  107.1 2.2 %collective-permute-done.9.right_ref = f32[2,16,128]{2,1,0:T(8,128)S(1)} collective-permute-done((f32[2,16,128]{2,1,0:T(8,128)S(1)}, f32[2,16,128]{2,1,0:T(8,128)S(1)}, u32[]{:S(2)}, u32[]{:S(2)}) %collective-permute-start.9) | collective-permute-done | bytes 16416 | tf_op jit(solution)/shard_map/ppermute | solution.py:106
  109.4 2.1 %collective-permute-start.10 = (f32[34,8,128]{2,1,0:T(8,128)S(1)}, f32[34,8,128]{2,1,0:T(8,128)S(1)}, u32[]{:S(2)}, u32[]{:S(2)}) collective-permute-start(f32[34,8,128]{2,1,0:T(8,128)S(1)} %get-tuple-element.20), channel_id=1, source_target_pairs={{0,4},{4,8},{8,12},{12,16},{16,20},{20,24},{24,28},{1,5},{5,9},{9,... | collective-permute-start | bytes 417800 | tf_op jit(solution)/shard_map/ppermute | solution.py:106
  111.5 4.5 %collective-permute-start.11 = (f32[34,8,128]{2,1,0:T(8,128)S(1)}, f32[34,8,128]{2,1,0:T(8,128)S(1)}, u32[]{:S(2)}, u32[]{:S(2)}) collective-permute-start(f32[34,8,128]{2,1,0:T(8,128)S(1)} %get-tuple-element.21), channel_id=1, source_target_pairs={{4,0},{8,4},{12,8},{16,12},{20,16},{24,20},{28,24},{5,1},{9,5},{13... | collective-permute-start | bytes 417800 | tf_op jit(solution)/shard_map/ppermute | solution.py:106
  116.0 2.2 %collective-permute-done.10.above_ref = f32[34,8,128]{2,1,0:T(8,128)S(1)} collective-permute-done((f32[34,8,128]{2,1,0:T(8,128)S(1)}, f32[34,8,128]{2,1,0:T(8,128)S(1)}, u32[]{:S(2)}, u32[]{:S(2)}) %collective-permute-start.10) | collective-permute-done | bytes 139296 | tf_op jit(solution)/shard_map/ppermute | solution.py:106
  118.6 7.8 %shard_map.68.grad_ref = f32[64,16,128]{2,1,0:T(8,128)S(1)} custom-call(s32[4]{0:T(128)S(1)} %pad_add_fusion.place_ref, f32[64]{0:T(128)S(1)} %copy-done.6, f32[64]{0:T(128)S(1)} %copy-done.7, f32[64,16,128]{2,1,0:T(8,128)S(1)} %get-tuple-element.16.x_ref.residual_ref, f32[2,16,128]{2,1,0:T(8,128)S(1)} %collective-permute-done.8.left_ref, ...), custom_call_target="tpu_custom_call" | custom-call | tf_op jit(solution)/shard_map/pallas_call | solution.py:27
  126.4 1.2 shard_map.69
  127.6 53.1 %all-gather.3.cloned.1.call-done = bf16[256,16,128]{2,1,0:T(8,128)(2,1)} async-done(((bf16[8,16,128]{2,1,0:T(8,128)(2,1)}), bf16[256,16,128]{2,1,0:T(8,128)(2,1)}) %all-gather.3.cloned.1.call-update) | async-done | bytes 1048592 | tf_op jit(solution)/shard_map/all_gather | solution.py:355
  180.7 1.2 copy-done.3
  181.9 2.8 %shard_map.70 = (f32[64,16,128]{2,1,0:T(8,128)}, f32[64,16,128]{2,1,0:T(8,128)}) custom-call(s32[4]{0:T(128)S(1)} %pad_add_fusion.place_ref, bf16[4,2,64,16,128]{4,3,2,1,0:T(8,128)(2,1)S(1)} %all-to-all-done.members_ref, f32[64,16,128]{2,1,0:T(8,128)S(1)} %get-tuple-element.16.x_ref.residual_ref, f32[64,16,128]{2,1,0:T(8,128)S(1)} %copy-done.5, ...), custom_call_target="tpu_custom_call" | custom-call | tf_op jit(solution)/shard_map/pallas_call | solution.py:27
  (26 shorter events, 2.0 us)
Async XLA Ops:
  7.2 1.6 copy-start.2
  9.4 1.3 copy-start
  10.7 5.3 %copy-start.1 = (f32[64,16,128]{2,1,0:T(8,128)S(1)}, f32[64,16,128]{2,1,0:T(8,128)}, u32[]{:S(2)}) copy-start(f32[64,16,128]{2,1,0:T(8,128)} %residual_ref.1) | copy-start | bytes 1572868
  10.7 60.6 %copy-start.6 = (f32[64]{0:T(128)S(1)}, f32[64]{0:T(128)}, u32[]{:S(2)}) copy-start(f32[64]{0:T(128)} %wx_ref.3) | copy-start | bytes 772
  10.7 60.6 %copy-start.7 = (f32[64]{0:T(128)S(1)}, f32[64]{0:T(128)}, u32[]{:S(2)}) copy-start(f32[64]{0:T(128)} %wy_ref.3) | copy-start | bytes 772
  10.7 68.4 %all-to-all-start = ((bf16[4,2,64,16,128]{4,3,2,1,0:T(8,128)(2,1)}), bf16[4,2,64,16,128]{4,3,2,1,0:T(8,128)(2,1)S(1)}, u32[]{:S(2)}, u32[]{:S(2)}) async-start(bf16[4,2,64,16,128]{4,3,2,1,0:T(8,128)(2,1)} %copy-done), calls=%async_computation | async-start | bytes 4194304 | tf_op jit(solution)/shard_map/all_to_all | solution.py:339
  16.0 164.7 %all-gather.3.cloned.1.call-start = ((), (), s32[]{:S(2)}) async-start(), calls=%async_computation.1 | async-start | bytes 1081344 | tf_op jit(solution)/shard_map/all_gather | solution.py:355
  16.4 45.9 %collective-permute-start = (f32[2,16,128]{2,1,0:T(8,128)S(1)}, f32[2,16,128]{2,1,0:T(8,128)S(1)}, u32[]{:S(2)}, u32[]{:S(2)}) collective-permute-start(f32[2,16,128]{2,1,0:T(8,128)S(1)} %get-tuple-element.12), channel_id=1, source_target_pairs={{0,1},{1,2},{2,3},{4,5},{5,6},{6,7},{8,9},{9,10},{10,11},{12,13},{... | collective-permute-start | bytes 49160 | tf_op jit(solution)/shard_map/ppermute | solution.py:106
  19.7 42.5 %collective-permute-start.1 = (f32[2,16,128]{2,1,0:T(8,128)S(1)}, f32[2,16,128]{2,1,0:T(8,128)S(1)}, u32[]{:S(2)}, u32[]{:S(2)}) collective-permute-start(f32[2,16,128]{2,1,0:T(8,128)S(1)} %get-tuple-element.13), channel_id=1, source_target_pairs={{1,0},{2,1},{3,2},{5,4},{6,5},{7,6},{9,8},{10,9},{11,10},{13,12},{... | collective-permute-start | bytes 49160 | tf_op jit(solution)/shard_map/ppermute | solution.py:106
  62.3 7.3 %collective-permute-start.2 = (f32[34,8,128]{2,1,0:T(8,128)S(1)}, f32[34,8,128]{2,1,0:T(8,128)S(1)}, u32[]{:S(2)}, u32[]{:S(2)}) collective-permute-start(f32[34,8,128]{2,1,0:T(8,128)S(1)} %get-tuple-element.14), channel_id=1, source_target_pairs={{0,4},{4,8},{8,12},{12,16},{16,20},{20,24},{24,28},{1,5},{5,9},{9,... | collective-permute-start | bytes 417800 | tf_op jit(solution)/shard_map/ppermute | solution.py:106
  64.2 7.1 %collective-permute-start.3 = (f32[34,8,128]{2,1,0:T(8,128)S(1)}, f32[34,8,128]{2,1,0:T(8,128)S(1)}, u32[]{:S(2)}, u32[]{:S(2)}) collective-permute-start(f32[34,8,128]{2,1,0:T(8,128)S(1)} %get-tuple-element.15), channel_id=1, source_target_pairs={{4,0},{8,4},{12,8},{16,12},{20,16},{24,20},{28,24},{5,1},{9,5},{13... | collective-permute-start | bytes 417800 | tf_op jit(solution)/shard_map/ppermute | solution.py:106
  79.7 6.7 %collective-permute-start.5 = (f32[8,16,128]{2,1,0:T(8,128)S(1)}, f32[8,16,128]{2,1,0:T(8,128)S(1)}, u32[]{:S(2)}, u32[]{:S(2)}) collective-permute-start(f32[8,16,128]{2,1,0:T(8,128)S(1)} %shard_map.63.mid_ref), channel_id=1, source_target_pairs={{1,0},{2,1},{3,2},{5,4},{6,5},{7,6},{9,8},{10,9},{11,10},{13,12},{... | collective-permute-start | bytes 196616 | tf_op jit(solution)/shard_map/ppermute | solution.py:106
  83.0 6.5 %collective-permute-start.4 = (f32[8,16,128]{2,1,0:T(8,128)S(1)}, f32[8,16,128]{2,1,0:T(8,128)S(1)}, u32[]{:S(2)}, u32[]{:S(2)}) collective-permute-start(f32[8,16,128]{2,1,0:T(8,128)S(1)} %shard_map.63.mid_ref), channel_id=1, source_target_pairs={{0,1},{1,2},{2,3},{4,5},{5,6},{6,7},{8,9},{9,10},{10,11},{12,13},{... | collective-permute-start | bytes 196616 | tf_op jit(solution)/shard_map/ppermute | solution.py:106
  89.8 4.9 %collective-permute-start.7 = (f32[8,16,128]{2,1,0:T(8,128)S(1)}, f32[8,16,128]{2,1,0:T(8,128)S(1)}, u32[]{:S(2)}, u32[]{:S(2)}) collective-permute-start(f32[8,16,128]{2,1,0:T(8,128)S(1)} %shard_map.64.mid_ref), channel_id=1, source_target_pairs={{4,0},{8,4},{12,8},{16,12},{20,16},{24,20},{28,24},{5,1},{9,5},{13... | collective-permute-start | bytes 196616 | tf_op jit(solution)/shard_map/ppermute | solution.py:106
  92.7 6.5 %collective-permute-start.6 = (f32[8,16,128]{2,1,0:T(8,128)S(1)}, f32[8,16,128]{2,1,0:T(8,128)S(1)}, u32[]{:S(2)}, u32[]{:S(2)}) collective-permute-start(f32[8,16,128]{2,1,0:T(8,128)S(1)} %shard_map.64.mid_ref), channel_id=1, source_target_pairs={{0,4},{4,8},{8,12},{12,16},{16,20},{20,24},{24,28},{1,5},{5,9},{9,... | collective-permute-start | bytes 196616 | tf_op jit(solution)/shard_map/ppermute | solution.py:106
  100.1 0.8 copy-start.4
  101.2 5.9 %collective-permute-start.8 = (f32[2,16,128]{2,1,0:T(8,128)S(1)}, f32[2,16,128]{2,1,0:T(8,128)S(1)}, u32[]{:S(2)}, u32[]{:S(2)}) collective-permute-start(f32[2,16,128]{2,1,0:T(8,128)S(1)} %get-tuple-element.18), channel_id=1, source_target_pairs={{0,1},{1,2},{2,3},{4,5},{5,6},{6,7},{8,9},{9,10},{10,11},{12,13},{... | collective-permute-start | bytes 49160 | tf_op jit(solution)/shard_map/ppermute | solution.py:106
  103.7 5.6 %collective-permute-start.9 = (f32[2,16,128]{2,1,0:T(8,128)S(1)}, f32[2,16,128]{2,1,0:T(8,128)S(1)}, u32[]{:S(2)}, u32[]{:S(2)}) collective-permute-start(f32[2,16,128]{2,1,0:T(8,128)S(1)} %get-tuple-element.19), channel_id=1, source_target_pairs={{1,0},{2,1},{3,2},{5,4},{6,5},{7,6},{9,8},{10,9},{11,10},{13,12},{... | collective-permute-start | bytes 49160 | tf_op jit(solution)/shard_map/ppermute | solution.py:106
  109.4 71.3 %copy-start.5 = (f32[64,16,128]{2,1,0:T(8,128)S(1)}, f32[64,16,128]{2,1,0:T(8,128)}, u32[]{:S(2)}) copy-start(f32[64,16,128]{2,1,0:T(8,128)} %copy-done.4) | copy-start | bytes 1572868
  109.4 8.8 %collective-permute-start.10 = (f32[34,8,128]{2,1,0:T(8,128)S(1)}, f32[34,8,128]{2,1,0:T(8,128)S(1)}, u32[]{:S(2)}, u32[]{:S(2)}) collective-permute-start(f32[34,8,128]{2,1,0:T(8,128)S(1)} %get-tuple-element.20), channel_id=1, source_target_pairs={{0,4},{4,8},{8,12},{12,16},{16,20},{20,24},{24,28},{1,5},{5,9},{9,... | collective-permute-start | bytes 417800 | tf_op jit(solution)/shard_map/ppermute | solution.py:106
  111.5 7.1 %collective-permute-start.11 = (f32[34,8,128]{2,1,0:T(8,128)S(1)}, f32[34,8,128]{2,1,0:T(8,128)S(1)}, u32[]{:S(2)}, u32[]{:S(2)}) collective-permute-start(f32[34,8,128]{2,1,0:T(8,128)S(1)} %get-tuple-element.21), channel_id=1, source_target_pairs={{4,0},{8,4},{12,8},{16,12},{20,16},{24,20},{28,24},{5,1},{9,5},{13... | collective-permute-start | bytes 417800 | tf_op jit(solution)/shard_map/ppermute | solution.py:106
  180.7 1.2 copy-start.3
Sparse Core Ops, SparseCore 0:
  127.7 52.9 all-gather.2
